TPU v7x, 32 devices: a whole 2x2x4 slice. The times are simulated.
32 devices in a mesh: visit: 4 (over y, core), patch: 8 (over z, x).
Axes of the slice: x: 2, y: 2, z: 4, core: 2. Of those that a mesh axis runs over, the one named last changes fastest.
Arguments:
- pieces: float32 [256, 512, 512], P(('visit', 'patch')), may hold values from -60 to 60
- ref_patch: float32 [8, 512, 512], P('patch', 'visit'), may hold values from -6 to 6
- piece_patch: int32 [256], P(('visit', 'patch')), may hold values from 0 to 7, as said below
- piece_visit: int32 [256], P(('visit', 'patch')), may hold values from 0 to 3, as said below
- anchors: int32 [256, 2], P(('visit', 'patch')), may hold values from 0 to 3584
- shifts: int32 [256, 2], P(('visit', 'patch')), may hold values from -2 to 2
- phases: float32 [256, 2], P(('visit', 'patch')), may hold values from 0 to 1
Outputs:
- matched: float32 [256, 512, 512], P(('visit', 'patch'))
- coefficients: float32 [16, 17, 17], P('visit')
Inputs may be any that keep to these rules, and one draw needn't show every extreme that they name: `piece_patch`: among the 8 pieces of one device at most 2 name the same patch; for each index of the visit axis one patch, drawn from the seed, is named by exactly 2 pieces of every device of that index. `piece_visit`: among the 8 pieces of one device each value occurs exactly 8 / 4 times.
All inputs are finite; a program needn't handle non-finite values.
Results may differ from a plain program's by a relative error of at most 0.0003.
Values sent between devices are 32-bit elements; how exact they have to be, the bound alone decides.
A program may use at most 192 MiB of HBM per device.

v0:
```python
import jax
import jax.numpy as jnp
from jax import lax
from jax.sharding import PartitionSpec as P

VIS_DEV = 4
TERMS = 17
TILE = 4096


exact_mode = lax.Precision.HIGHEST


def lanczos_batch(band_shift, sub_phase, side_len):
    positions = jnp.arange(side_len, dtype=jnp.int32)
    whole = positions[None, :, None] + band_shift[:, None, None] - positions[None, None, :]
    offset = whole.astype(sub_phase.dtype) + sub_phase[:, None, None]
    weight = jnp.sinc(offset) * jnp.sinc(offset / 3.0)
    return jnp.where(jnp.abs(offset) < 3.0, weight, jnp.zeros_like(weight))


def warp_batch(slab_images, row_shift, col_shift, row_phase, col_phase):
    side_len = slab_images.shape[1]
    left_matrix = lanczos_batch(row_shift, row_phase, side_len)
    middle = jnp.einsum("kia,kab->kib", left_matrix, slab_images, precision=exact_mode)
    right_matrix = lanczos_batch(col_shift, col_phase, side_len)
    return jnp.einsum("kib,kjb->kij", middle, right_matrix, precision=exact_mode)


def chebyshev_rows(first_pixel, side_len):
    pixels = (first_pixel + jnp.arange(side_len, dtype=jnp.int32)).astype(jnp.float32)
    coordinate = (2.0 * pixels + 1.0) / TILE - 1.0
    orders = jnp.arange(TERMS, dtype=jnp.int32).astype(jnp.float32)
    return jnp.cos(orders[:, None] * jnp.arccos(coordinate)[None, :])


def basis_pair(anchor_pairs, side_len):
    row_basis = jax.vmap(lambda first_pixel: chebyshev_rows(first_pixel, side_len))(
        anchor_pairs[:, 0]
    )
    col_basis = jax.vmap(lambda first_pixel: chebyshev_rows(first_pixel, side_len))(
        anchor_pairs[:, 1]
    )
    return (row_basis, col_basis)


def project_terms(differences, anchor_pairs):
    row_basis, col_basis = basis_pair(anchor_pairs, differences.shape[1])
    middle = jnp.einsum("mtp,mpq->mtq", row_basis, differences, precision=exact_mode)
    return jnp.einsum("mtq,muq->mtu", middle, col_basis, precision=exact_mode)


def body(pieces, ref_patch, piece_patch, piece_visit, anchors, shifts, phases):
    piece_count = pieces.shape[0]
    side_len = pieces.shape[1]
    patch_count = lax.axis_size("patch")
    full_ref = lax.all_gather(ref_patch, "visit", axis=1, tiled=True)
    visit_slots = jnp.arange(VIS_DEV, dtype=jnp.int32)
    own_onehot = (piece_visit[:, None] == visit_slots[None, :]).astype(jnp.float32)
    warped_all = warp_batch(pieces, shifts[:, 0], shifts[:, 1], phases[:, 0], phases[:, 1])
    ref_block = lax.all_gather(full_ref, "patch", axis=0, tiled=True)
    block_count = ref_block.shape[0]
    match_table = (
        piece_patch[:, None] == jnp.arange(block_count, dtype=jnp.int32)[None, :]
    ).astype(jnp.float32)
    own_diffs = warped_all - jnp.einsum("kb,bij->kij", match_table, ref_block, precision=exact_mode)
    partial_value = project_terms(own_diffs, anchors)
    local_sums = jnp.einsum("kv,ktu->vtu", own_onehot, partial_value, precision=exact_mode)
    totals = lax.psum(local_sums, "patch")
    coefficients = totals / float(patch_count * (piece_count // VIS_DEV) * side_len * side_len)
    row_basis, col_basis = basis_pair(anchors, side_len)
    chosen = jnp.einsum("kv,vtu->ktu", own_onehot, coefficients, precision=exact_mode)
    middle = jnp.einsum("ktp,ktu->kpu", row_basis, chosen, precision=exact_mode)
    fitted = jnp.einsum("kpu,kuq->kpq", middle, col_basis, precision=exact_mode)
    return (own_diffs - fitted, coefficients)


def solution(mesh):
    return jax.shard_map(
        body,
        mesh=mesh,
        in_specs=(
            P(("visit", "patch"), None, None),
            P("patch", "visit", None),
            P(("visit", "patch")),
            P(("visit", "patch")),
            P(("visit", "patch"), None),
            P(("visit", "patch"), None),
            P(("visit", "patch"), None),
        ),
        out_specs=(P(("visit", "patch"), None, None), P("visit", None, None)),
        check_vma=False,
    )
```

profile of v0, /device:TPU:0, one launch (start us, length us, event | category | flops | bytes accessed | tf_op | source)
XLA Modules:
  0.0 243.1 jit_solution(2393528352477433763)
XLA Ops:
  7.2 0.0 all-gather.3.cloned.1.call-start
  7.2 1.9 copy.11
  9.1 0.0 all-gather.3.cloned.1.call-update
  9.2 0.0 all-gather.5.cloned.1.call-start
  9.2 20.4 %all-gather.3.cloned.1.call-done = f32[1,512,512]{2,0,1:T(1,128)} async-done(((f32[1,128,512]{2,0,1:T(1,128)}), f32[1,512,512]{2,0,1:T(1,128)}) %all-gather.3.cloned.1.call-update) | async-done | bytes 1048592 | tf_op jit(solution)/shard_map/all_gather | solution.py:57
  29.6 2.4 copy.12
  32.0 0.0 all-gather.5.cloned.1.call-update
  32.0 0.8 slice_bitcast_fusion.3
  32.8 0.8 slice_bitcast_fusion.2
  33.5 0.8 slice_bitcast_fusion
  34.3 0.1 iota_add_fusion.1
  34.3 0.1 iota_add_fusion
  34.4 0.7 sqrt_atan2_fusion
  35.2 37.1 %fusion.64 = f32[8,512,512]{2,1,0:T(8,128)S(1)} fusion(f32[8,512,512]{2,1,0:T(8,128)} %param.8, f32[8]{0:T(128)S(1)} %get-tuple-element.8, s32[8,512]{1,0:T(8,128)S(1)} %iota_add_fusion.1), kind=kOutput, calls=%fused_computation.110 | convolution fusion | flops 13037993984 | bytes 16793632 | tf_op jit(solution)/shard_map/kia,kab->kib/dot_general | solution.py:25
  72.3 39.2 %fusion.59 = f32[8,512,512]{2,1,0:T(8,128)} fusion(f32[8,512,512]{2,1,0:T(8,128)S(1)} %fusion.64, f32[8]{0:T(128)S(1)} %get-tuple-element.7, s32[8,512]{1,0:T(8,128)S(1)} %iota_add_fusion), kind=kOutput, calls=%fused_computation.105 | convolution fusion | flops 13037993984 | bytes 16793632 | tf_op jit(solution)/shard_map/kib,kjb->kij/dot_general | solution.py:27
  111.5 45.6 %all-gather.5.cloned.1.call-done = f32[8,512,512]{2,1,0:T(8,128)} async-done(((f32[1,512,512]{2,1,0:T(8,128)}), f32[8,512,512]{2,1,0:T(8,128)}) %all-gather.5.cloned.1.call-update) | async-done | bytes 8388624 | tf_op jit(solution)/shard_map/all_gather | solution.py:61
  157.1 13.6 %fusion.32 = f32[8,512,512]{2,0,1:T(8,128)S(1)} fusion(f32[8,512,512]{2,1,0:T(8,128)} %all-gather.5.cloned.1.call-done, s32[8]{0:T(128)S(1)} %copy-done.5), kind=kOutput, calls=%fused_computation.61 | convolution fusion | flops 201326656 | bytes 16777248 | tf_op jit(solution)/shard_map/kb,bij->kij/dot_general | solution.py:66
  170.8 9.3 %fusion.100 = f32[8,17,512]{2,1,0:T(8,128)S(1)} fusion(f32[8,512,512]{2,1,0:T(8,128)S(1)} %copy-done.1, f32[8,512,512]{2,0,1:T(8,128)S(1)} %fusion.32, f32[8,512]{1,0:T(8,128)S(1)} %get-tuple-element.10, f32[17]{0:T(128)S(1)} %iota_convert_fusion), kind=kOutput, calls=%fused_computation.142 | convolution fusion | flops 429985792 | bytes 17072196 | tf_op jit(solution)/shard_map/mtp,mpq->mtq/dot_general | solution.py:49
  180.1 1.8 fusion.101
  182.0 0.2 fusion.112
  182.1 34.7 %psum.7 = f32[4,17,17]{2,0,1:T(4,128)S(1)} all-reduce(f32[4,17,17]{2,0,1:T(4,128)S(1)} %fusion.112), channel_id=1, replica_groups=mesh['visit'=4,'patch'=8] {'patch'}, use_global_device_ids=true, to_apply=%region_0.2 | all-reduce | flops 1156 | bytes 9248 | tf_op jit(solution)/shard_map/psum | solution.py:69
  216.9 0.2 fusion.118
  217.1 2.3 fusion.102
  219.5 16.8 %convolution_subtract_fusion = f32[8,512,512]{2,1,0:T(8,128)} fusion(f32[8,512,17]{1,2,0:T(8,128)S(1)} %fusion.102, f32[8,512,512]{2,1,0:T(8,128)} %fusion.59, f32[8,512,512]{2,0,1:T(8,128)} %copy-done, f32[8,512]{1,0:T(8,128)S(1)} %copy-done.2, f32[17]{0:T(128)S(1)} %iota_convert_fusion), kind=kOutput, calls=%fused_computation.141 | convolution fusion | flops 432082944 | bytes 25460804 | tf_op jit(solution)/shard_map/kpu,kuq->kpq/dot_general | solution.py:74
  (14 shorter events, 0.0 us)
Async XLA Ops:
  7.2 22.4 %all-gather.3.cloned.1.call-start = ((), (), s32[]{:S(2)}) async-start(), calls=%async_computation | async-start | bytes 1310720 | tf_op jit(solution)/shard_map/all_gather | solution.py:57
  9.2 147.9 %all-gather.5.cloned.1.call-start = ((), (), s32[]{:S(2)}) async-start(), calls=%async_computation.1 | async-start | bytes 9437184 | tf_op jit(solution)/shard_map/all_gather | solution.py:61
  72.3 84.8 %copy-start.5 = (s32[8]{0:T(128)S(1)}, s32[8]{0:T(128)}, u32[]{:S(2)}) copy-start(s32[8]{0:T(128)} %param.10) | copy-start | bytes 100
  157.1 13.6 %copy-start.1 = (f32[8,512,512]{2,1,0:T(8,128)S(1)}, f32[8,512,512]{2,1,0:T(8,128)}, u32[]{:S(2)}) copy-start(f32[8,512,512]{2,1,0:T(8,128)} %fusion.59) | copy-start | bytes 25165828
  170.7 9.4 %copy-start = (f32[8,512,512]{2,0,1:T(8,128)}, f32[8,512,512]{2,0,1:T(8,128)S(1)}, u32[]{:S(2)}) copy-start(f32[8,512,512]{2,0,1:T(8,128)S(1)} %fusion.32) | copy-start | bytes 25165828
  170.7 9.4 %copy-start.2 = (f32[8,512]{1,0:T(8,128)S(1)}, f32[8,512]{1,0:T(8,128)}, u32[]{:S(2)}) copy-start(f32[8,512]{1,0:T(8,128)} %get-tuple-element.9) | copy-start | bytes 49156
  170.7 11.2 %copy-start.4 = (s32[8]{0:T(128)S(1)}, s32[8]{0:T(128)}, u32[]{:S(2)}) copy-start(s32[8]{0:T(128)} %param.11) | copy-start | bytes 100
  216.9 19.4 %copy-start.3 = (f32[4,17,17]{2,0,1:T(4,128)}, f32[4,17,17]{2,0,1:T(4,128)S(1)}, u32[]{:S(2)}) copy-start(f32[4,17,17]{2,0,1:T(4,128)S(1)} %broadcast_multiply_fusion) | copy-start | bytes 13876
Sparse Core Ops, SparseCore 0:
  10.1 19.4 all-gather.2
  32.1 124.9 all-gather.4
where the time goes:
time: 243 us
  matrix products  121 us (50%)
  waiting for transfers between devices  66 us (27%)
  blocking collectives  34.7 us (14%)
  between operations  14.2 us (6%)
  local copies, waits for them, and re-layouts  6.59 us (3%)
    all_gather x1, waiting for transfers between devices, body(): ref_block = lax.all_gather(full_ref, 'patch', axis=0, tiled=True)  45.6 us
    dot_general x1, matrix products, warp_batch(): jnp.einsum('kib,kjb->kij', middle, right_matrix, precision=exact_mode)  39.2 us
    dot_general x1, matrix products, warp_batch(): jnp.einsum('kia,kab->kib', left_matrix, slab_images, precision=exact_mode)  37.1 us
    psum x1, blocking collectives, body(): totals = lax.psum(local_sums, 'patch')  34.7 us
    all_gather x1, waiting for transfers between devices, body(): full_ref = lax.all_gather(ref_patch, 'visit', axis=1, tiled=True)  20.4 us
    dot_general x1, matrix products, body(): fitted = jnp.einsum('kpu,kuq->kpq', middle, col_basis, precision=exact_mode)  16.8 us
    dot_general x1, matrix products, body(): jnp.einsum('kb,bij->kij', match_table, ref_block, precision=exact_mode)  13.6 us
    dot_general x1, matrix products, project_terms(): jnp.einsum('mtp,mpq->mtq', row_basis, differences, precision=exact_mode)  9.34 us
  transfers between devices with their start and end apart: 2, of which 2 were waited for; matrix products, arithmetic and copies ran while one was open for 33% of the time, Pallas kernels for 0%

commit v1 on v0

v1 whole, which is shorter than its diff:
```python
import functools
import itertools

import jax
import jax.numpy as jnp
from jax import lax
from jax.experimental import pallas as pl
from jax.experimental.pallas import tpu as pltpu
from jax.sharding import PartitionSpec as P

VIS_DEV = 4
TERMS = 17
TILE = 4096
TAPS = 6
LINE = 4
TROWS = 32
BLOCK = 128
MESH = pl.DeviceIdType.MESH
exact_mode = lax.Precision.HIGHEST
bf16 = jnp.bfloat16
f32 = jnp.float32


def split(x):
    hi = x.astype(bf16)
    return hi, (x - hi.astype(f32)).astype(bf16)


def mm(a, b):
    return jnp.dot(a, b, preferred_element_type=f32)


def tap_weights(phases):
    offset = jnp.arange(-3, TAPS - 3, dtype=jnp.int32).astype(f32)[None, None, :] + phases[:, :, None]
    weight = jnp.sinc(offset) * jnp.sinc(offset / 3.0)
    weight = jnp.where(jnp.abs(offset) < 3.0, weight, jnp.zeros_like(weight))
    return weight.reshape(phases.shape[0], 2 * TAPS)


def fill_basis(anchor_ref, rows, cols, side):
    count = anchor_ref.shape[0]
    pixel = lax.broadcasted_iota(jnp.int32, (count, side), 1)
    for ref, axis in ((rows, 0), (cols, 1)):
        ref[...] = jnp.zeros(ref.shape, f32)
        first = anchor_ref[:, axis : axis + 1]
        u = (2.0 * (first + pixel).astype(f32) + 1.0) / TILE - 1.0
        before, now = jnp.ones_like(u), u
        ref[:, 0, :] = before
        for m in range(1, TERMS):
            ref[:, m, :] = now
            before, now = now, 2.0 * u * now - before


def pick(index, values):
    out = jnp.int32(values[0])
    for place in range(1, len(values)):
        out = jnp.where(index == place, jnp.int32(values[place]), out)
    return out


def nearest(size, rank):
    return [sorted(range(size), key=lambda j: (abs(j - i), j))[rank] for i in range(size)]


class Gather:
    def __init__(self, sizes, parts, rows):
        self.sizes, self.parts, self.rows = sizes, parts, rows
        self.chips = sizes[0] * sizes[1] * sizes[2]
        self.sends = 0
        self.events = []
        offset = 0
        for number, (height, order) in enumerate(parts):
            for ranks in itertools.product(*(range(n) for n in sizes)):
                self.events.append((sum(ranks), number, ranks, offset, height, order))
            offset += height
        self.events.sort(key=lambda e: (e[0], e[1]))
        slots = []
        for _, number, ranks, offset, height, order in self.events:
            stage = max([-1] + [j for j in range(3) if ranks[order[j]]])
            kinds = []
            if stage >= 0 and sizes[order[stage]] > 2:
                kinds.append(("on", order[stage]))
            for axis in order[stage + 1 :]:
                kinds += [("up", axis), ("down", axis)] if sizes[axis] > 2 else [("swap", axis)]
            kinds.append(("core", 0))
            slots.append([(kind, axis, self.sends + j) for j, (kind, axis) in enumerate(kinds)])
            self.sends += len(kinds)
        self.slots = slots

    def bind(self, buffer, send_sem, recv_sem, core_sem):
        sa, sb, sy = self.sizes
        place, visit = lax.axis_index("patch"), lax.axis_index("visit")
        self.me = (place // sb, place % sb, visit // 2)
        self.core = visit % 2
        self.buffer, self.send_sem, self.recv_sem, self.core_sem = buffer, send_sem, recv_sem, core_sem

    def device(self, coords, core):
        return (coords[2] * 2 + core, coords[0] * self.sizes[1] + coords[1])

    def source(self, ranks):
        return [
            self.me[j] if ranks[j] == 0 else pick(self.me[j], nearest(self.sizes[j], ranks[j]))
            for j in range(3)
        ]

    def view(self, at, core, offset, height):
        start = pl.multiple_of((at[2] * 2 + core) * self.rows + offset, 8)
        return self.buffer.at[at[0] * self.sizes[1] + at[1], pl.ds(start, height), :]

    def index(self, number, at):
        return number * self.chips + (at[0] * self.sizes[1] + at[1]) * self.sizes[2] + at[2]

    def copies(self, event):
        _, number, ranks, offset, height, _ = self.events[event]
        at = self.source(ranks)
        view = self.view(at, self.core, offset, height)
        index = self.index(number, at)
        for kind, axis, slot in self.slots[event]:
            to, valid, sem, core = list(self.me), None, self.recv_sem, self.core
            if kind == "core":
                sem, core = self.core_sem, 1 - self.core
            elif kind == "swap":
                to[axis] = 1 - self.me[axis]
            else:
                if kind == "on":
                    step = jnp.where(at[axis] < self.me[axis], 1, -1)
                else:
                    step = 1 if kind == "up" else -1
                to[axis] = self.me[axis] + step
                valid = jnp.logical_and(to[axis] >= 0, to[axis] < self.sizes[axis])
            yield valid, pltpu.make_async_remote_copy(
                src_ref=view,
                dst_ref=view,
                send_sem=self.send_sem.at[slot],
                recv_sem=sem.at[index],
                device_id=self.device(to, core),
                device_id_type=MESH,
            )

    def each(self, event, act):
        for valid, copy in self.copies(event):
            if valid is None:
                act(copy)
            else:
                pl.when(valid)(functools.partial(act, copy))

    def arrive(self, event, core):
        _, number, ranks, offset, height, _ = self.events[event]
        at = self.source(ranks)
        owner = 1 - self.core if core else self.core
        view = self.view(at, owner, offset, height)
        sem = self.core_sem if core else self.recv_sem
        pltpu.make_async_remote_copy(
            src_ref=view,
            dst_ref=view,
            send_sem=self.send_sem.at[0],
            recv_sem=sem.at[self.index(number, at)],
            device_id=self.device(self.me, 1 - self.core),
            device_id_type=MESH,
        ).wait_recv()

    def run(self, event):
        if sum(self.events[event][2]):
            self.arrive(event, False)
        self.each(event, lambda copy: copy.start())

    def finish(self):
        for event in range(len(self.events)):
            self.arrive(event, True)

    def drain(self):
        for event in range(len(self.events)):
            self.each(event, lambda copy: copy.wait_send())


def greet(gather, patch_total):
    barrier = pltpu.get_barrier_semaphore()
    place, visit = lax.axis_index("patch"), lax.axis_index("visit")
    ny = gather.sizes[2]
    y, core = gather.me[2], gather.core

    def call(device):
        pl.semaphore_signal(barrier, inc=1, device_id=device, device_id_type=MESH)

    call((y * 2 + 1 - core, place))
    for step in (1, -1):
        pl.when(jnp.logical_and(y + step >= 0, y + step < ny))(
            lambda step=step: call(((y + step) * 2 + core, place))
        )
    for shift in range(1, patch_total):
        call((visit, (place + shift) % patch_total))
    beside = jnp.where(y > 0, 1, 0) + jnp.where(y < ny - 1, 1, 0)
    pl.semaphore_wait(barrier, patch_total + beside)


def fit_kernel(
    gather,
    patch_total,
    scale,
    pieces,
    ref_patch,
    anchors,
    piece_patch,
    piece_visit,
    shifts,
    weights,
    diff_out,
    coef_out,
    work,
    everyone,
    xhi,
    xlo,
    strip,
    rhi,
    rlo,
    vrow,
    vcol,
    sums,
    gathered,
    in_sem,
    out_sem,
    own_sem,
    send_sem,
    recv_sem,
    core_sem,
    sum_send,
    sum_recv,
):
    count, side = work.shape[0], work.shape[1]
    pad = BLOCK // 2
    place, visit = lax.axis_index("patch"), lax.axis_index("visit")
    gather.bind(everyone, send_sem, recv_sem, core_sem)

    start = pl.multiple_of(visit * gather.rows, 8)
    own = pltpu.make_async_copy(
        ref_patch.at[0], everyone.at[place, pl.ds(start, gather.rows), :], own_sem
    )
    own.start()
    for k in range(count):
        pltpu.make_async_copy(pieces.at[k], work.at[k], in_sem.at[k]).start()
    greet(gather, patch_total)
    own.wait()
    local = [e for e in range(len(gather.events)) if sum(gather.events[e][2]) == 0]
    for event in local:
        gather.run(event)

    fill_basis(anchors, vrow, vcol, side)
    for ref in (xhi, xlo):
        ref[0:pad, :] = jnp.zeros((pad, side), bf16)
        ref[pad + side : 2 * pad + side, :] = jnp.zeros((pad, side), bf16)
    for ref in (rhi, rlo):
        ref[...] = jnp.zeros((side, side), bf16)
    sums[...] = jnp.zeros_like(sums)

    blocks = side // BLOCK
    ticks = count * blocks
    remote = [e for e in range(len(gather.events)) if sum(gather.events[e][2])]

    def banded(k, axis, distance):
        out = jnp.zeros(distance.shape, f32)
        for tap in range(TAPS):
            out = jnp.where(distance == tap - 3, weights[k, axis * TAPS + tap], out)
        return split(out)

    def prepare(k):
        pltpu.make_async_copy(pieces.at[k], work.at[k], in_sem.at[k]).wait()
        for q in range(blocks):
            hi, lo = split(work[k, q * BLOCK : (q + 1) * BLOCK, :])
            xhi[pad + q * BLOCK : pad + (q + 1) * BLOCK, :] = hi
            xlo[pad + q * BLOCK : pad + (q + 1) * BLOCK, :] = lo
        shape = (BLOCK, 2 * BLOCK)
        d = lax.broadcasted_iota(jnp.int32, shape, 0) - lax.broadcasted_iota(jnp.int32, shape, 1)
        hi, lo = banded(k, 0, d + pad + shifts[k, 0])
        strip[0:BLOCK, :] = hi
        strip[BLOCK : 2 * BLOCK, :] = lo
        shape = (BLOCK, BLOCK)
        d = lax.broadcasted_iota(jnp.int32, shape, 1) - lax.broadcasted_iota(jnp.int32, shape, 0)
        for step in (-1, 0, 1):
            hi, lo = banded(k, 1, d + step * BLOCK + shifts[k, 1])
            for i in range(blocks):
                j = i + step
                if 0 <= j < blocks:
                    rhi[i * BLOCK : (i + 1) * BLOCK, j * BLOCK : (j + 1) * BLOCK] = hi
                    rlo[i * BLOCK : (i + 1) * BLOCK, j * BLOCK : (j + 1) * BLOCK] = lo

    @pl.loop(0, ticks)
    def _(t):
        k, q = t // blocks, t % blocks
        pl.when(q == 0)(lambda: prepare(k))
        base = pl.multiple_of(q * BLOCK, BLOCK)
        window = pl.ds(base, 2 * BLOCK)
        both = mm(strip[...], xhi[window, :])
        middle = both[:BLOCK] + both[BLOCK:] + mm(strip[0:BLOCK, :], xlo[window, :])
        hi, lo = split(middle)
        both = mm(jnp.concatenate([hi, lo], 0), rhi[...])
        work[k, pl.ds(base, BLOCK), :] = both[:BLOCK] + both[BLOCK:] + mm(hi, rlo[...])
        for tick in range(ticks):
            due = [e for n, e in enumerate(remote) if (n * ticks) // len(remote) == tick]
            if due:
                pl.when(t == tick)(lambda due=due: [gather.run(e) for e in due] and None)

    gather.finish()

    half = side // 2

    @pl.loop(0, count)
    def _(k):
        patch_id = piece_patch[k]
        hi, lo = split(vrow[k])
        stacked = jnp.concatenate([hi, lo], 0)
        total = jnp.zeros((TROWS, side), f32)
        for h in range(2):
            rows = slice(h * half, (h + 1) * half)
            diff = work[k, rows, :] - everyone[patch_id, rows, :]
            work[k, rows, :] = diff
            dhi, dlo = split(diff)
            both = mm(stacked[:, rows], dhi)
            total = total + both[:TROWS] + both[TROWS:] + mm(hi[:, rows], dlo)
        pltpu.make_async_copy(work.at[k], diff_out.at[k], out_sem.at[k]).start()
        columns = vcol[k]
        spread = jnp.concatenate(
            [jnp.where(piece_visit[k] == v, columns, 0.0) for v in range(VIS_DEV)], 0
        )
        sums[...] += lax.dot_general(
            total, spread, (((1,), (1,)), ((), ())), precision=exact_mode, preferred_element_type=f32
        )

    def exchange(shift):
        return pltpu.make_async_remote_copy(
            src_ref=sums,
            dst_ref=gathered.at[place],
            send_sem=sum_send.at[shift],
            recv_sem=sum_recv.at[place],
            device_id=(visit, (place + shift) % patch_total),
            device_id_type=MESH,
        )

    for shift in range(1, patch_total):
        exchange(shift).start()
    gathered[place] = sums[...]
    gather.drain()
    for shift in range(1, patch_total):
        origin = (place + shift) % patch_total
        pltpu.make_async_remote_copy(
            src_ref=sums,
            dst_ref=gathered.at[origin],
            send_sem=sum_send.at[shift],
            recv_sem=sum_recv.at[origin],
            device_id=(visit, origin),
            device_id_type=MESH,
        ).wait_recv()
    total = gathered[0]
    for origin in range(1, patch_total):
        total = total + gathered[origin]
    coef_out[...] = total / scale
    for shift in range(1, patch_total):
        exchange(shift).wait_send()
    for k in range(count):
        pltpu.make_async_copy(work.at[k], diff_out.at[k], out_sem.at[k]).wait()


def subtract_kernel(piece_visit, diff, coef, anchors, out, vrow, vcol):
    k = pl.program_id(0)
    side = diff.shape[1]
    pl.when(k == 0)(lambda: fill_basis(anchors, vrow, vcol, side))
    chosen = coef[piece_visit[k]]
    inner = jnp.dot(chosen, vcol[k], precision=exact_mode, preferred_element_type=f32)
    ihi, ilo = split(inner)
    rhi, rlo = split(vrow[k])
    fit = lax.dot_general(
        jnp.concatenate([rhi, rhi, rlo], 0),
        jnp.concatenate([ihi, ilo, ihi], 0),
        (((0,), (0,)), ((), ())),
        preferred_element_type=f32,
    )
    out[0] = diff[0] - fit


def body(nv, pieces, ref_patch, piece_patch, piece_visit, anchors, shifts, phases):
    count, side = pieces.shape[0], pieces.shape[1]
    patch_total = lax.axis_size("patch")
    rows = ref_patch.shape[1]
    sizes = (LINE, patch_total // LINE, nv // 2)
    parts = [(rows // 2, (0, 1, 2)), (rows // 2, (0, 2, 1))]
    gather = Gather(sizes, parts, rows)
    weights = tap_weights(phases)
    scale = float(patch_total * (count // VIS_DEV) * side * side)
    anywhere = pl.BlockSpec(memory_space=pl.ANY)
    vmem = pl.BlockSpec(memory_space=pltpu.VMEM)
    smem = pl.BlockSpec(memory_space=pltpu.SMEM)
    lanes = VIS_DEV * TROWS
    dma = pltpu.SemaphoreType.DMA
    diff, sums = pl.pallas_call(
        functools.partial(fit_kernel, gather, patch_total, scale),
        out_shape=(
            jax.ShapeDtypeStruct(pieces.shape, f32),
            jax.ShapeDtypeStruct((TROWS, lanes), f32),
        ),
        in_specs=[anywhere, anywhere, vmem, smem, smem, smem, smem],
        out_specs=(anywhere, vmem),
        scratch_shapes=[
            pltpu.VMEM((count, side, side), f32),
            pltpu.VMEM((patch_total, side, side), f32),
            pltpu.VMEM((side + BLOCK, side), bf16),
            pltpu.VMEM((side + BLOCK, side), bf16),
            pltpu.VMEM((2 * BLOCK, 2 * BLOCK), bf16),
            pltpu.VMEM((side, side), bf16),
            pltpu.VMEM((side, side), bf16),
            pltpu.VMEM((count, TROWS, side), f32),
            pltpu.VMEM((count, TROWS, side), f32),
            pltpu.VMEM((TROWS, lanes), f32),
            pltpu.VMEM((patch_total, TROWS, lanes), f32),
            dma((count,)),
            dma((count,)),
            dma,
            dma((gather.sends,)),
            dma((len(parts) * gather.chips,)),
            dma((len(parts) * gather.chips,)),
            dma((patch_total,)),
            dma((patch_total,)),
        ],
        compiler_params=pltpu.CompilerParams(
            collective_id=0, has_side_effects=True, vmem_limit_bytes=48 * 2**20
        ),
        name="gather_warp_project",
    )(pieces, ref_patch, anchors, piece_patch, piece_visit, shifts, weights)
    table = sums.reshape(TROWS, VIS_DEV, TROWS).transpose(1, 0, 2)
    matched = pl.pallas_call(
        subtract_kernel,
        out_shape=jax.ShapeDtypeStruct(pieces.shape, f32),
        grid=(count,),
        in_specs=[
            smem,
            pl.BlockSpec((1, side, side), lambda k: (k, 0, 0)),
            pl.BlockSpec((VIS_DEV, TROWS, TROWS), lambda k: (0, 0, 0)),
            pl.BlockSpec((count, 2), lambda k: (0, 0)),
        ],
        out_specs=pl.BlockSpec((1, side, side), lambda k: (k, 0, 0)),
        scratch_shapes=[
            pltpu.VMEM((count, TROWS, side), f32),
            pltpu.VMEM((count, TROWS, side), f32),
        ],
        compiler_params=pltpu.CompilerParams(vmem_limit_bytes=32 * 2**20),
        name="subtract_fit",
    )(piece_visit, diff, table, anchors)
    return matched, table[:, :TERMS, :TERMS]


def solution(mesh):
    return jax.shard_map(
        functools.partial(body, mesh.shape["visit"]),
        mesh=mesh,
        in_specs=(
            P(("visit", "patch"), None, None),
            P("patch", "visit", None),
            P(("visit", "patch")),
            P(("visit", "patch")),
            P(("visit", "patch"), None),
            P(("visit", "patch"), None),
            P(("visit", "patch"), None),
        ),
        out_specs=(P(("visit", "patch"), None, None), P("visit", None, None)),
        check_vma=False,
    )
```

time: 243 us -> 80.4 us (0.33)
  matrix products: 121 us -> 0 us
  Pallas kernels: 0 us -> 70.5 us
  waiting for transfers between devices: 66 us -> 0 us
  blocking collectives: 34.7 us -> 0 us
  between operations: 14.2 us -> 0.69 us
    dot_general x9 -> x0, matrix products: 121 us -> none  [the longest x1 39.2 us: warp_batch(): jnp.einsum('kib,kjb->kij', middle, right_matrix, precision=exact_mode)]
    pallas_call x0 -> x2, Pallas kernels: none -> 70.5 us  [the longest x1 63.5 us: body(): pl.pallas_call(functools.partial(fit_kernel, gather, patch_total, scale),...]
    all_gather x2 -> x0, waiting for transfers between devices: 66 us -> none  [the longest x1 45.6 us: body(): ref_block = lax.all_gather(full_ref, 'patch', axis=0, tiled=True)]
    psum x1 -> x0, blocking collectives: 34.7 us -> none  [body(): totals = lax.psum(local_sums, 'patch')]
    unnamed x13 -> x14, local copies, waits for them, and re-layouts: 1.96 us -> 8.53 us
  transfers between devices with their start and end apart: 2 -> 0, of which waited for: 2 -> 0; matrix products, arithmetic and copies ran while one was open for 33% -> 0% of each run, Pallas kernels for 0% -> 0%
where the time goes in v1:
time: 80.4 us; the launch traced here: 80.1 us
  Pallas kernels  70.5 us (88%)
  local copies, waits for them, and re-layouts  8.71 us (11%)
    pallas_call x1, Pallas kernels, body(): pl.pallas_call(functools.partial(fit_kernel, gather, patch_total, scale),...  63.5 us
    unnamed x14, local copies, waits for them, and re-layouts  8.53 us
    pallas_call x1, Pallas kernels, body(): pl.pallas_call(subtract_kernel, out_shape=jax.ShapeDtypeStruct(pieces.sha...  7.07 us

profile of v1, /device:TPU:0, one launch (start us, length us, event | category | flops | bytes accessed | tf_op | source)
XLA Modules:
  0.0 80.1 jit_solution(10511201513895668193)
XLA Ops:
  0.6 0.0 copy-start.3
  0.7 0.8 copy.15.anchors
  1.4 0.8 copy.16.shifts
  2.2 0.8 copy.14
  2.9 0.2 compare_select_fusion.6
  3.1 0.1 reshape.16.weights
  3.2 0.0 copy-start.1
  3.2 1.0 %copy-done.1 = f32[1,128,512]{2,1,0:T(8,128)S(1)} copy-done((f32[1,128,512]{2,1,0:T(8,128)S(1)}, f32[1,128,512]{2,1,0:T(8,128)}, u32[]{:S(2)}) %copy-start.1) | copy-done | bytes 262168
  4.1 0.0 copy-start.2
  4.1 0.7 copy-done.2
  4.8 0.0 copy-start.4
  4.8 0.7 copy-done.4
  5.4 63.5 %gather_warp_project.1 = (f32[8,512,512]{2,1,0:T(8,128)}, f32[32,128]{1,0:T(8,128)S(1)}) custom-call(f32[8,512,512]{2,1,0:T(8,128)} %pieces.1, f32[1,128,512]{2,1,0:T(8,128)S(1)} %copy-done.1, s32[8,2]{1,0:T(8,128)S(1)} %copy.15.anchors, s32[8]{0:T(128)S(1)} %copy-done.4, s32[8]{0:T(128)S(1)} %copy-done.2, s32[8,2]{1,0:T(8,128)S(1)} %copy.16.shifts, ...), custom_call_target="tpu_custom_call" | custom-call | tf_op jit(solution)/shard_map/gather_warp_project/pallas_call | solution.py:393
  68.9 0.1 reshape.17
  69.0 0.0 copy-done.3
  69.0 0.0 copy-start
  69.0 3.4 %copy-done = f32[8,512,512]{2,1,0:T(8,128)S(1)} copy-done((f32[8,512,512]{2,1,0:T(8,128)S(1)}, f32[8,512,512]{2,1,0:T(8,128)}, u32[]{:S(2)}) %copy-start) | copy-done | bytes 8388632
  72.4 7.1 %subtract_fit.1 = f32[8,512,512]{2,1,0:T(8,128)} custom-call(s32[8]{0:T(128)S(1)} %copy-done.3, f32[8,512,512]{2,1,0:T(8,128)S(1)} %copy-done, f32[4,32,32]{2,1,0:T(8,128)S(1)} %bitcast.3, s32[8,2]{1,0:T(8,128)S(1)} %copy.15.anchors), custom_call_target="tpu_custom_call" | custom-call | tf_op jit(solution)/shard_map/subtract_fit/pallas_call | solution.py:428
  79.5 0.6 copy.19
  (3 shorter events, 0.0 us)
Async XLA Ops:
  0.6 68.4 %copy-start.3 = (s32[8]{0:T(128)S(1)}, s32[8]{0:T(128)}, u32[]{:S(2)}) copy-start(s32[8]{0:T(128)} %piece_visit.3) | copy-start | bytes 100
  3.2 1.0 %copy-start.1 = (f32[1,128,512]{2,1,0:T(8,128)S(1)}, f32[1,128,512]{2,1,0:T(8,128)}, u32[]{:S(2)}) copy-start(f32[1,128,512]{2,1,0:T(8,128)} %ref_patch.1) | copy-start | bytes 786436
  4.1 0.7 copy-start.2
  4.8 0.7 copy-start.4
  69.0 3.4 %copy-start = (f32[8,512,512]{2,1,0:T(8,128)S(1)}, f32[8,512,512]{2,1,0:T(8,128)}, u32[]{:S(2)}) copy-start(f32[8,512,512]{2,1,0:T(8,128)} %get-tuple-element.5.diff) | copy-start | bytes 25165828

commit v2 on v1

--- a/solution.py
+++ b/solution.py
@@ -15,6 +15,7 @@
 LINE = 4
 TROWS = 32
 BLOCK = 128
+PARTS = ((4, (0, 1, 2)), (4, (0, 2, 1)))
 MESH = pl.DeviceIdType.MESH
 exact_mode = lax.Precision.HIGHEST
 bf16 = jnp.bfloat16
@@ -31,18 +32,21 @@
 
 
 def tap_weights(phases):
-    offset = jnp.arange(-3, TAPS - 3, dtype=jnp.int32).astype(f32)[None, None, :] + phases[:, :, None]
+    offset = jnp.arange(-3, TAPS - 3, dtype=jnp.int32).astype(f32)[None, :, None] + phases.T[:, None, :]
     weight = jnp.sinc(offset) * jnp.sinc(offset / 3.0)
     weight = jnp.where(jnp.abs(offset) < 3.0, weight, jnp.zeros_like(weight))
-    return weight.reshape(phases.shape[0], 2 * TAPS)
+    return weight.reshape(2 * TAPS, phases.shape[0])
 
 
 def fill_basis(anchor_ref, rows, cols, side):
-    count = anchor_ref.shape[0]
+    count = anchor_ref.shape[1]
+    piece = lax.broadcasted_iota(jnp.int32, (count, side), 0)
     pixel = lax.broadcasted_iota(jnp.int32, (count, side), 1)
     for ref, axis in ((rows, 0), (cols, 1)):
         ref[...] = jnp.zeros(ref.shape, f32)
-        first = anchor_ref[:, axis : axis + 1]
+        first = jnp.zeros((count, side), jnp.int32)
+        for k in range(count):
+            first = jnp.where(piece == k, anchor_ref[axis, k], first)
         u = (2.0 * (first + pixel).astype(f32) + 1.0) / TILE - 1.0
         before, now = jnp.ones_like(u), u
         ref[:, 0, :] = before
@@ -206,6 +210,8 @@
     weights,
     diff_out,
     coef_out,
+    left_out,
+    vcol_out,
     work,
     everyone,
     xhi,
@@ -215,10 +221,14 @@
     rlo,
     vrow,
     vcol,
+    left,
+    chi,
+    clo,
     sums,
     gathered,
     in_sem,
     out_sem,
+    basis_sem,
     own_sem,
     send_sem,
     recv_sem,
@@ -245,6 +255,27 @@
         gather.run(event)
 
     fill_basis(anchors, vrow, vcol, side)
+
+    @pl.loop(0, count)
+    def _(k):
+        hi, lo = split(vrow[k])
+        hi = hi.astype(f32)
+        stack = jnp.concatenate([hi, hi, lo.astype(f32), jnp.zeros_like(hi)], 0)
+        left[k] = stack.T.astype(bf16)
+        columns = vcol[k]
+        spread = jnp.concatenate(
+            [jnp.where(piece_visit[k] == v, columns, 0.0) for v in range(VIS_DEV)], 0
+        )
+        hi, lo = split(spread)
+        chi[k] = hi.astype(f32).T.astype(bf16)
+        clo[k] = lo.astype(f32).T.astype(bf16)
+
+    basis = [
+        pltpu.make_async_copy(left, left_out, basis_sem.at[0]),
+        pltpu.make_async_copy(vcol, vcol_out, basis_sem.at[1]),
+    ]
+    for copy in basis:
+        copy.start()
     for ref in (xhi, xlo):
         ref[0:pad, :] = jnp.zeros((pad, side), bf16)
         ref[pad + side : 2 * pad + side, :] = jnp.zeros((pad, side), bf16)
@@ -259,7 +290,7 @@
     def banded(k, axis, distance):
         out = jnp.zeros(distance.shape, f32)
         for tap in range(TAPS):
-            out = jnp.where(distance == tap - 3, weights[k, axis * TAPS + tap], out)
+            out = jnp.where(distance == tap - 3, weights[axis * TAPS + tap, k], out)
         return split(out)
 
     def prepare(k):
@@ -270,13 +301,13 @@
             xlo[pad + q * BLOCK : pad + (q + 1) * BLOCK, :] = lo
         shape = (BLOCK, 2 * BLOCK)
         d = lax.broadcasted_iota(jnp.int32, shape, 0) - lax.broadcasted_iota(jnp.int32, shape, 1)
-        hi, lo = banded(k, 0, d + pad + shifts[k, 0])
+        hi, lo = banded(k, 0, d + pad + shifts[0, k])
         strip[0:BLOCK, :] = hi
         strip[BLOCK : 2 * BLOCK, :] = lo
         shape = (BLOCK, BLOCK)
         d = lax.broadcasted_iota(jnp.int32, shape, 1) - lax.broadcasted_iota(jnp.int32, shape, 0)
         for step in (-1, 0, 1):
-            hi, lo = banded(k, 1, d + step * BLOCK + shifts[k, 1])
+            hi, lo = banded(k, 1, d + step * BLOCK + shifts[1, k])
             for i in range(blocks):
                 j = i + step
                 if 0 <= j < blocks:
@@ -295,7 +326,7 @@
         both = mm(jnp.concatenate([hi, lo], 0), rhi[...])
         work[k, pl.ds(base, BLOCK), :] = both[:BLOCK] + both[BLOCK:] + mm(hi, rlo[...])
         for tick in range(ticks):
-            due = [e for n, e in enumerate(remote) if (n * ticks) // len(remote) == tick]
+            due = [e for n, e in enumerate(remote) if ticks // 7 + (n * (ticks - ticks // 7)) // len(remote) == tick]
             if due:
                 pl.when(t == tick)(lambda due=due: [gather.run(e) for e in due] and None)
 
@@ -317,13 +348,9 @@
             both = mm(stacked[:, rows], dhi)
             total = total + both[:TROWS] + both[TROWS:] + mm(hi[:, rows], dlo)
         pltpu.make_async_copy(work.at[k], diff_out.at[k], out_sem.at[k]).start()
-        columns = vcol[k]
-        spread = jnp.concatenate(
-            [jnp.where(piece_visit[k] == v, columns, 0.0) for v in range(VIS_DEV)], 0
-        )
-        sums[...] += lax.dot_general(
-            total, spread, (((1,), (1,)), ((), ())), precision=exact_mode, preferred_element_type=f32
-        )
+        thi, tlo = split(total)
+        both = mm(jnp.concatenate([thi, tlo], 0), chi[k])
+        sums[...] += both[:TROWS] + both[TROWS:] + mm(thi, clo[k])
 
     def exchange(shift):
         return pltpu.make_async_remote_copy(
@@ -352,28 +379,31 @@
     total = gathered[0]
     for origin in range(1, patch_total):
         total = total + gathered[origin]
-    coef_out[...] = total / scale
+    total = total / scale
+    for v in range(VIS_DEV):
+        coef_out[v] = total[:, v * TROWS : (v + 1) * TROWS]
+    for copy in basis:
+        copy.wait()
     for shift in range(1, patch_total):
         exchange(shift).wait_send()
     for k in range(count):
         pltpu.make_async_copy(work.at[k], diff_out.at[k], out_sem.at[k]).wait()
 
 
-def subtract_kernel(piece_visit, diff, coef, anchors, out, vrow, vcol):
+def subtract_kernel(piece_visit, diff, coef, left, vcol, out, right):
     k = pl.program_id(0)
-    side = diff.shape[1]
-    pl.when(k == 0)(lambda: fill_basis(anchors, vrow, vcol, side))
-    chosen = coef[piece_visit[k]]
-    inner = jnp.dot(chosen, vcol[k], precision=exact_mode, preferred_element_type=f32)
-    ihi, ilo = split(inner)
-    rhi, rlo = split(vrow[k])
-    fit = lax.dot_general(
-        jnp.concatenate([rhi, rhi, rlo], 0),
-        jnp.concatenate([ihi, ilo, ihi], 0),
-        (((0,), (0,)), ((), ())),
-        preferred_element_type=f32,
-    )
-    out[0] = diff[0] - fit
+    count = piece_visit.shape[0]
+
+    def prepare(j, slot):
+        inner = jnp.dot(
+            coef[piece_visit[j]], vcol[j], precision=exact_mode, preferred_element_type=f32
+        )
+        hi, lo = split(inner)
+        right[slot] = jnp.concatenate([hi, lo, hi, jnp.zeros_like(hi)], 0)
+
+    pl.when(k == 0)(lambda: prepare(0, 0))
+    out[0] = diff[0] - mm(left[0], right[k % 2])
+    prepare(jnp.minimum(k + 1, count - 1), (k + 1) % 2)
 
 
 def body(nv, pieces, ref_patch, piece_patch, piece_visit, anchors, shifts, phases):
@@ -381,7 +411,7 @@
     patch_total = lax.axis_size("patch")
     rows = ref_patch.shape[1]
     sizes = (LINE, patch_total // LINE, nv // 2)
-    parts = [(rows // 2, (0, 1, 2)), (rows // 2, (0, 2, 1))]
+    parts = [(rows * eighths // 8, order) for eighths, order in PARTS]
     gather = Gather(sizes, parts, rows)
     weights = tap_weights(phases)
     scale = float(patch_total * (count // VIS_DEV) * side * side)
@@ -390,14 +420,16 @@
     smem = pl.BlockSpec(memory_space=pltpu.SMEM)
     lanes = VIS_DEV * TROWS
     dma = pltpu.SemaphoreType.DMA
-    diff, sums = pl.pallas_call(
+    diff, table, left, vcol = pl.pallas_call(
         functools.partial(fit_kernel, gather, patch_total, scale),
         out_shape=(
             jax.ShapeDtypeStruct(pieces.shape, f32),
-            jax.ShapeDtypeStruct((TROWS, lanes), f32),
+            jax.ShapeDtypeStruct((VIS_DEV, TROWS, TROWS), f32),
+            jax.ShapeDtypeStruct((count, side, 4 * TROWS), bf16),
+            jax.ShapeDtypeStruct((count, TROWS, side), f32),
         ),
-        in_specs=[anywhere, anywhere, vmem, smem, smem, smem, smem],
-        out_specs=(anywhere, vmem),
+        in_specs=[anywhere, anywhere, smem, smem, smem, smem, smem],
+        out_specs=(anywhere, vmem, anywhere, anywhere),
         scratch_shapes=[
             pltpu.VMEM((count, side, side), f32),
             pltpu.VMEM((patch_total, side, side), f32),
@@ -408,10 +440,14 @@
             pltpu.VMEM((side, side), bf16),
             pltpu.VMEM((count, TROWS, side), f32),
             pltpu.VMEM((count, TROWS, side), f32),
+            pltpu.VMEM((count, side, 4 * TROWS), bf16),
+            pltpu.VMEM((count, side, lanes), bf16),
+            pltpu.VMEM((count, side, lanes), bf16),
             pltpu.VMEM((TROWS, lanes), f32),
             pltpu.VMEM((patch_total, TROWS, lanes), f32),
             dma((count,)),
             dma((count,)),
+            dma((2,)),
             dma,
             dma((gather.sends,)),
             dma((len(parts) * gather.chips,)),
@@ -420,11 +456,10 @@
             dma((patch_total,)),
         ],
         compiler_params=pltpu.CompilerParams(
-            collective_id=0, has_side_effects=True, vmem_limit_bytes=48 * 2**20
+            collective_id=0, has_side_effects=True, vmem_limit_bytes=60 * 2**20
         ),
         name="gather_warp_project",
-    )(pieces, ref_patch, anchors, piece_patch, piece_visit, shifts, weights)
-    table = sums.reshape(TROWS, VIS_DEV, TROWS).transpose(1, 0, 2)
+    )(pieces, ref_patch, anchors.T, piece_patch, piece_visit, shifts.T, weights)
     matched = pl.pallas_call(
         subtract_kernel,
         out_shape=jax.ShapeDtypeStruct(pieces.shape, f32),
@@ -433,16 +468,14 @@
             smem,
             pl.BlockSpec((1, side, side), lambda k: (k, 0, 0)),
             pl.BlockSpec((VIS_DEV, TROWS, TROWS), lambda k: (0, 0, 0)),
-            pl.BlockSpec((count, 2), lambda k: (0, 0)),
+            pl.BlockSpec((1, side, 4 * TROWS), lambda k: (k, 0, 0)),
+            pl.BlockSpec((count, TROWS, side), lambda k: (0, 0, 0)),
         ],
         out_specs=pl.BlockSpec((1, side, side), lambda k: (k, 0, 0)),
-        scratch_shapes=[
-            pltpu.VMEM((count, TROWS, side), f32),
-            pltpu.VMEM((count, TROWS, side), f32),
-        ],
-        compiler_params=pltpu.CompilerParams(vmem_limit_bytes=32 * 2**20),
+        scratch_shapes=[pltpu.VMEM((2, 4 * TROWS, side), bf16)],
+        compiler_params=pltpu.CompilerParams(vmem_limit_bytes=60 * 2**20),
         name="subtract_fit",
-    )(piece_visit, diff, table, anchors)
+    )(piece_visit, diff, table, left, vcol)
     return matched, table[:, :TERMS, :TERMS]
 
 

time: 80.4 us -> 75.4 us (0.938)
  local copies, waits for them, and re-layouts: 8.71 us -> 2.15 us
  Pallas kernels: 70.5 us -> 72 us
    unnamed x14 -> x3, local copies, waits for them, and re-layouts: 8.53 us -> 0.63 us
    pallas_call x1, Pallas kernels: 7.07 us -> 10.2 us  [body(): pl.pallas_call(subtract_kernel, out_shape=jax.ShapeDtypeStruct(pieces.sha...]
    pallas_call x1, Pallas kernels: 63.5 us -> 61.8 us  [body(): pl.pallas_call(functools.partial(fit_kernel, gather, patch_total, scale),...]
where the time goes in v2:
time: 75.4 us; the launch traced here: 75 us
  Pallas kernels  72 us (95%)
  local copies, waits for them, and re-layouts  2.15 us (3%)
    pallas_call x1, Pallas kernels, body(): pl.pallas_call(functools.partial(fit_kernel, gather, patch_total, scale),...  61.8 us
    pallas_call x1, Pallas kernels, body(): pl.pallas_call(subtract_kernel, out_shape=jax.ShapeDtypeStruct(pieces.sha...  10.2 us

profile of v2, /device:TPU:0, one launch (start us, length us, event | category | flops | bytes accessed | tf_op | source)
XLA Modules:
  0.0 75.0 jit_solution(13242244254629731381)
XLA Ops:
  0.6 0.8 %copy.12 = f32[2,8]{0,1:T(8,128)S(1)} copy(f32[2,8]{1,0:T(2,128)} %bitcast.7) | data formatting | bytes 128 | tf_op jit(solution)/shard_map/transpose | solution.py:35
  1.4 0.2 compare_select_fusion.6
  1.6 0.1 reshape.13
  1.6 0.7 copy.13.weights
  2.3 61.8 %gather_warp_project.1 = (f32[8,512,512]{2,1,0:T(8,128)}, f32[4,32,32]{2,1,0:T(8,128)}, bf16[8,512,128]{2,1,0:T(8,128)(2,1)}, f32[8,32,512]{2,1,0:T(8,128)}) custom-call(f32[8,512,512]{2,1,0:T(8,128)} %pieces.1, f32[1,128,512]{2,1,0:T(8,128)} %ref_patch.1, s32[2,8]{1,0:T(2,128)} %bitcast.5, s32[8]{0:T(128)} %piece_patch.1, s32[8]{0:T(128)} %piece_visit.3, ...), custom_call_target="tpu_custom_call" | custom-call | tf_op jit(solution)/shard_map/gather_warp_project/pallas_call | solution.py:423
  64.1 0.0 copy-start
  64.1 10.2 %subtract_fit.1 = f32[8,512,512]{2,1,0:T(8,128)} custom-call(s32[8]{0:T(128)} %piece_visit.3, f32[8,512,512]{2,1,0:T(8,128)} %get-tuple-element.7.diff, f32[4,32,32]{2,1,0:T(8,128)} %get-tuple-element.8.coef, bf16[8,512,128]{2,1,0:T(8,128)(2,1)} %get-tuple-element.9.left, f32[8,32,512]{2,1,0:T(8,128)} %get-tuple-element.10.vcol), custom_call_target="tpu_custom_call" | custom-call | tf_op jit(solution)/shard_map/subtract_fit/pallas_call | solution.py:463
  74.3 0.0 copy-done
  74.3 0.6 copy.14
  (2 shorter events, 0.0 us)
Async XLA Ops:
  64.1 10.2 %copy-start = (f32[4,32,32]{2,1,0:T(8,128)S(1)}, f32[4,32,32]{2,1,0:T(8,128)}, u32[]{:S(2)}) copy-start(f32[4,32,32]{2,1,0:T(8,128)} %get-tuple-element.8.coef) | copy-start | bytes 49156

commit v3 on v2

--- a/solution.py
+++ b/solution.py
@@ -77,7 +77,7 @@
             for ranks in itertools.product(*(range(n) for n in sizes)):
                 self.events.append((sum(ranks), number, ranks, offset, height, order))
             offset += height
-        self.events.sort(key=lambda e: (e[0], e[1]))
+        self.events.sort(key=lambda e: (e[0], -e[2][0], e[1]))
         slots = []
         for _, number, ranks, offset, height, order in self.events:
             stage = max([-1] + [j for j in range(3) if ranks[order[j]]])

time: 75.4 us -> 74.2 us (0.984)
  Pallas kernels: 72 us -> 70.9 us
    pallas_call x1, Pallas kernels: 61.8 us -> 60.6 us  [body(): pl.pallas_call(functools.partial(fit_kernel, gather, patch_total, scale),...]
where the time goes in v3:
time: 74.2 us; the launch traced here: 73.8 us
  Pallas kernels  70.9 us (96%)
  local copies, waits for them, and re-layouts  2.15 us (3%)
    pallas_call x1, Pallas kernels, body(): pl.pallas_call(functools.partial(fit_kernel, gather, patch_total, scale),...  60.6 us
    pallas_call x1, Pallas kernels, body(): pl.pallas_call(subtract_kernel, out_shape=jax.ShapeDtypeStruct(pieces.sha...  10.2 us

profile of v3, /device:TPU:0, one launch (start us, length us, event | category | flops | bytes accessed | tf_op | source)
XLA Modules:
  0.0 73.8 jit_solution(17268939087823637005)
XLA Ops:
  0.6 0.8 %copy.12 = f32[2,8]{0,1:T(8,128)S(1)} copy(f32[2,8]{1,0:T(2,128)} %bitcast.7) | data formatting | bytes 128 | tf_op jit(solution)/shard_map/transpose | solution.py:35
  1.4 0.2 compare_select_fusion.6
  1.6 0.1 reshape.13
  1.6 0.7 copy.13.weights
  2.3 60.6 %gather_warp_project.1 = (f32[8,512,512]{2,1,0:T(8,128)}, f32[4,32,32]{2,1,0:T(8,128)}, bf16[8,512,128]{2,1,0:T(8,128)(2,1)}, f32[8,32,512]{2,1,0:T(8,128)}) custom-call(f32[8,512,512]{2,1,0:T(8,128)} %pieces.1, f32[1,128,512]{2,1,0:T(8,128)} %ref_patch.1, s32[2,8]{1,0:T(2,128)} %bitcast.5, s32[8]{0:T(128)} %piece_patch.1, s32[8]{0:T(128)} %piece_visit.3, ...), custom_call_target="tpu_custom_call" | custom-call | tf_op jit(solution)/shard_map/gather_warp_project/pallas_call | solution.py:423
  63.0 0.0 copy-start
  63.0 10.2 %subtract_fit.1 = f32[8,512,512]{2,1,0:T(8,128)} custom-call(s32[8]{0:T(128)} %piece_visit.3, f32[8,512,512]{2,1,0:T(8,128)} %get-tuple-element.7.diff, f32[4,32,32]{2,1,0:T(8,128)} %get-tuple-element.8.coef, bf16[8,512,128]{2,1,0:T(8,128)(2,1)} %get-tuple-element.9.left, f32[8,32,512]{2,1,0:T(8,128)} %get-tuple-element.10.vcol), custom_call_target="tpu_custom_call" | custom-call | tf_op jit(solution)/shard_map/subtract_fit/pallas_call | solution.py:463
  73.2 0.0 copy-done
  73.2 0.6 copy.14
  (2 shorter events, 0.0 us)
Async XLA Ops:
  63.0 10.2 %copy-start = (f32[4,32,32]{2,1,0:T(8,128)S(1)}, f32[4,32,32]{2,1,0:T(8,128)}, u32[]{:S(2)}) copy-start(f32[4,32,32]{2,1,0:T(8,128)} %get-tuple-element.8.coef) | copy-start | bytes 49156
